TPU v7x, 32 devices: a whole 2x2x4 slice. The times are simulated.
32 devices in a mesh: seq: 8 (over y, x, core), head: 4 (over z).
Axes of the slice: x: 2, y: 2, z: 4, core: 2. Of those that a mesh axis runs over, the one named last changes fastest.
Arguments:
- head_inputs: bfloat16 [2, 4096, 8192], P(None, 'seq', 'head'), may hold values from -6 to 6
- gate_inputs: bfloat16 [2, 4096, 8192], P(None, 'seq', 'head'), may hold values from -6 to 6
- state_writes: bfloat16 [2, 4096, 1024], P(None, 'seq', 'head'), may hold values from -6 to 6
- state_reads: bfloat16 [2, 4096, 1024], P(None, 'seq', 'head'), may hold values from -6 to 6
- step_raw: float32 [2, 128, 4096], P(None, 'head', 'seq'), may hold values from -4 to 4
- decay_log: float32 [128], P('head')
- conv_inputs: float32 [4, 8192], P(None, 'head'), may hold values from -3 to 3
- conv_writes: float32 [4, 1024], P(None, 'head'), may hold values from -3 to 3
- conv_reads: float32 [4, 1024], P(None, 'head'), may hold values from -3 to 3
- norm_gain: float32 [8192], P('head'), may hold values from 0.1 to 1.9
- out_weight: bfloat16 [8192, 8192], P('head', 'seq'), may hold values from -0.0625 to 0.0625
Outputs:
- mixed: bfloat16 [2, 4096, 8192], P(None, 'seq', 'head')
All inputs are finite; a program needn't handle non-finite values.
Results may differ from a plain program's by a relative error of at most 0.017.
Values may be sent and summed in bfloat16 or wider, within the bound.
A program may use at most 128 MiB of HBM per device.

v0:
```python
import jax
import jax.numpy as jnp
from jax import lax
from jax.sharding import PartitionSpec as P

HEAD_DIM = 64
STATE = 128
CONV = 4
SPAN = 128


HIGH = lax.Precision.HIGHEST


def shifted(value, axis, steps):
    count = lax.axis_size(axis)
    initial, last = (max(0, -steps), min(count, count - steps))
    return lax.ppermute(value, axis, [(source, source + steps) for source in range(initial, last)])


def causal_conv(local, rim, weight):
    length = local.shape[1]
    joined = jnp.concatenate([rim, local], axis=1).astype(jnp.float32)
    total = weight[0] * joined[:, 0:length]
    for tap in range(1, CONV):
        total = total + weight[tap] * joined[:, tap : tap + length]
    return jax.nn.silu(total)


def per_device(
    head_inputs,
    gate_inputs,
    state_writes,
    state_reads,
    step_raw,
    decay_log,
    conv_inputs,
    conv_writes,
    conv_reads,
    norm_gain,
    out_weight,
):
    seqs, length, width = head_inputs.shape
    heads = decay_log.shape[0]
    groups = state_writes.shape[2] // STATE
    per_group = heads // groups
    spans = length // SPAN
    rim = CONV - 1
    rims = shifted(
        (
            head_inputs[:, length - rim :],
            state_writes[:, length - rim :],
            state_reads[:, length - rim :],
        ),
        "seq",
        1,
    )
    values = causal_conv(head_inputs, rims[0], conv_inputs)
    writes = causal_conv(state_writes, rims[1], conv_writes)
    reads = causal_conv(state_reads, rims[2], conv_reads)
    steps = jax.nn.softplus(step_raw)
    log_decay = steps * (-jnp.exp(decay_log))[None, :, None]
    steps_blocks = steps.reshape(seqs, heads, spans, SPAN)
    cumul = jnp.cumsum(log_decay.reshape(seqs, heads, spans, SPAN), axis=-1)
    values_blocks = values.reshape(seqs, spans, SPAN, groups, per_group, HEAD_DIM)
    writes_blocks = writes.reshape(seqs, spans, SPAN, groups, STATE)
    reads_blocks = reads.reshape(seqs, spans, SPAN, groups, STATE)
    scores = jnp.einsum("scign,scjgn->sgcij", reads_blocks, writes_blocks, precision=HIGH)
    later = jnp.arange(SPAN)[:, None] >= jnp.arange(SPAN)[None, :]
    gaps = jnp.where(later, cumul[..., :, None] - cumul[..., None, :], -jnp.inf)
    mixing = jnp.exp(gaps) * steps_blocks[..., None, :]
    mixing = mixing.reshape(seqs, groups, per_group, spans, SPAN, SPAN) * scores[:, :, None]
    diagonal = jnp.einsum("sghcij,scjghp->scighp", mixing, values_blocks, precision=HIGH)
    weights_in = (jnp.exp(cumul[..., -1:] - cumul) * steps_blocks).reshape(
        seqs, groups, per_group, spans, SPAN
    )
    block_states = jnp.einsum(
        "scjgn,sghcj,scjghp->sghcnp", writes_blocks, weights_in, values_blocks, precision=HIGH
    )
    block_states = block_states.reshape(seqs, heads, spans, STATE, HEAD_DIM)
    block_decay = jnp.exp(cumul[..., -1])
    entering = [jnp.zeros((seqs, heads, STATE, HEAD_DIM), jnp.float32)]
    leading = [jnp.ones((seqs, heads), jnp.float32)]
    for index in range(spans):
        entering.append(
            block_decay[:, :, index, None, None] * entering[-1] + block_states[:, :, index]
        )
        leading.append(leading[-1] * block_decay[:, :, index])
    final_state = entering[spans]
    device_logs = jnp.sum(log_decay, axis=-1)
    all_logs = lax.all_gather(device_logs[None], "seq", axis=0, tiled=True)
    before = jnp.cumsum(all_logs, axis=0) - all_logs
    own_index = lax.axis_index("seq")
    own_before = lax.dynamic_index_in_dim(before, own_index, 0, keepdims=False)
    piece = lax.all_gather(
        final_state[None].astype(jnp.bfloat16), "seq", axis=0, tiled=True
    ).astype(jnp.float32)
    count = piece.shape[0]
    source = jnp.arange(count, dtype=jnp.int32)
    far_gaps = jnp.where(
        (source < own_index)[:, None, None], own_before[None] - before - all_logs, -jnp.inf
    )
    carried = jnp.zeros_like(final_state) + jnp.sum(
        jnp.exp(far_gaps)[..., None, None] * piece, axis=0
    )
    entering_all = (
        jnp.stack(entering[:spans], axis=2)
        + jnp.stack(leading[:spans], axis=2)[..., None, None] * carried[:, :, None]
    )
    entering_all = entering_all.reshape(seqs, groups, per_group, spans, STATE, HEAD_DIM)
    scale_in = jnp.exp(cumul).reshape(seqs, groups, per_group, spans, SPAN).transpose(0, 3, 4, 1, 2)
    reading = (
        jnp.einsum("scign,sghcnp->scighp", reads_blocks, entering_all, precision=HIGH)
        * scale_in[..., None]
    )
    ssd_out = (diagonal + reading).reshape(seqs, length, width)
    gated = ssd_out * jax.nn.silu(gate_inputs.astype(jnp.float32))
    grouped = gated.reshape(seqs, length, groups, width // groups)
    normed = grouped * lax.rsqrt(jnp.mean(grouped * grouped, axis=-1, keepdims=True) + 1e-05)
    normed = (normed.reshape(seqs, length, width) * norm_gain).astype(jnp.bfloat16)
    token_rows = normed.reshape(seqs * length, width)
    partial_out = jnp.dot(
        token_rows,
        lax.all_gather(out_weight, "seq", axis=1, tiled=True),
        preferred_element_type=jnp.float32,
    )
    mixed = lax.psum_scatter(
        partial_out.astype(jnp.bfloat16), "head", scatter_dimension=1, tiled=True
    ).astype(jnp.float32)
    return mixed.astype(jnp.bfloat16).reshape(seqs, length, mixed.shape[1])


def solution(mesh):
    return jax.shard_map(
        per_device,
        mesh=mesh,
        in_specs=(
            P(None, "seq", "head"),
            P(None, "seq", "head"),
            P(None, "seq", "head"),
            P(None, "seq", "head"),
            P(None, "head", "seq"),
            P("head"),
            P(None, "head"),
            P(None, "head"),
            P(None, "head"),
            P("head"),
            P("head", "seq"),
        ),
        out_specs=P(None, "seq", "head"),
        check_vma=False,
    )
```

profile of v0, /device:TPU:0, one launch (start us, length us, event | category | flops | bytes accessed | tf_op | source)
XLA Modules:
  0.0 628.7 jit_solution(1779966534289710037)
XLA Ops:
  7.5 2.4 collective-permute-start
  10.6 4.5 collective-permute-start.2
  16.7 1.1 multiply_reduce_fusion.1
  17.8 2.3 reduce_window_sum.22
  21.5 6.2 copy.63
  29.6 4.7 maximum_convert_fusion
  34.3 9.5 %divide_multiply_fusion = f32[2,512,2048]{1,2,0:T(8,128)} fusion(f32[2,515,2048]{1,2,0:T(8,128)S(1)} %maximum_convert_fusion, f32[2048]{0:T(1024)S(1)} %bitcast.124, f32[2048]{0:T(1024)S(1)} %bitcast.125, f32[2048]{0:T(1024)S(1)} %bitcast.123, f32[2048]{0:T(1024)S(1)} %bitcast.122), kind=kLoop, calls=%fused_computation.43 | loop fusion | flops 23068672 | bytes 41975808 | tf_op jit(solution)/shard_map/jit(silu)/mul | solution.py:27
  43.8 9.9 %reshape.146 = f32[2,4,128,2,16,64]{2,1,5,4,3,0:T(4,128)} reshape(f32[2,512,2048]{1,2,0:T(8,128)} %divide_multiply_fusion) | data formatting | bytes 16777216 | tf_op jit(solution)/shard_map/reshape | solution.py:65
  53.7 10.4 %broadcast_multiply_fusion = f32[2,4,128,2,16,64]{2,1,5,4,3,0:T(4,128)} fusion(f32[2,4,128,2,16,64]{2,1,5,4,3,0:T(4,128)} %reshape.146, f32[2,4,128,2,16]{2,1,4,3,0:T(4,128)S(1)} %copy.70), kind=kLoop, calls=%fused_computation.49 | loop fusion | flops 2097152 | bytes 16908288 | tf_op jit(solution)/shard_map/scjgn,sghcj,scjghp->sghcnp/dot_general | solution.py:77
  64.1 11.1 %fusion.35 = f32[2,2,16,4,128,64]{4,5,2,3,1,0:T(8,128)S(1)} fusion(f32[2,4,128,2,16,64]{2,1,5,4,3,0:T(4,128)} %broadcast_multiply_fusion, f32[2,4,128,2,128,1]{4,3,2,1,0,5:T(2,128)S(1)} %bitcast.113), kind=kOutput, calls=%fused_computation.50 | convolution fusion | flops 3221225472 | bytes 17825792 | tf_op jit(solution)/shard_map/scjgn,sghcj,scjghp->sghcnp/dot_general | solution.py:77
  75.2 1.7 copy.73
  76.9 3.2 copy-done.1
  80.1 1.7 fusion.43
  82.6 1.9 collective-permute-start.1
  84.6 8.9 %all-gather.1 = f32[8,2,32]{2,1,0:T(2,128)S(1)} all-gather(f32[1,2,32]{2,1,0:T(2,128)S(1)} %bitcast.132), channel_id=2, replica_groups=mesh['seq'=8,'head'=4] {'seq'}, dimensions={0}, use_global_device_ids=true | all-gather | bytes 2304 | tf_op jit(solution)/shard_map/all_gather | solution.py:91
  95.0 6.6 %copy.82 = bf16[2,512,2048]{1,2,0:T(8,128)(2,1)} copy(bf16[2,512,2048]{2,1,0:T(8,128)(2,1)} %param.12) | data formatting | bytes 8388608 | tf_op args[1]
  102.9 2.3 fusion.55
  105.2 6.6 %bitcast_add_fusion.3 = (f32[2,32,1,128,64]{3,4,1,0,2:T(8,128)}, f32[2,32,1,128,64]{3,4,1,0,2:T(8,128)}, f32[2,32,1,128,64]{3,4,1,0,2:T(8,128)}) fusion(f32[2,32,4,128,64]{3,4,2,1,0:T(8,128)} %bitcast.109, f32[2,32]{1,0:T(2,128)} %bitcast.129, f32[2,32]{1,0:T(2,128)} %bitcast.131, f32[2,32]{1,0:T(2,128)S(1)} %bitcast.127), kind=kLoop, calls=%fused_computation.60 | loop fusion | flops 2621440 | bytes 12583680 | tf_op jit(solution)/shard_map/add | solution.py:86
  111.8 24.9 %all-gather.5.cloned.1.call-done = bf16[8,2,32,128,64]{3,4,2,1,0:T(8,128)(2,1)} async-done(((bf16[1,2,32,128,64]{3,4,2,1,0:T(8,128)(2,1)}), bf16[8,2,32,128,64]{3,4,2,1,0:T(8,128)(2,1)}) %all-gather.5.cloned.1.call-update) | async-done | bytes 8388624 | tf_op jit(solution)/shard_map/all_gather | solution.py:95
  136.7 5.4 multiply_reduce_fusion
  142.1 9.4 %fusion.13 = f32[2,4,2,16,64,128]{5,4,3,2,1,0:T(8,128)S(1)} fusion(f32[2,2,16,1,128,64]{4,5,2,1,3,0:T(8,128)S(1)} %bitcast.115, f32[2,2,16,1,128,64]{4,5,2,1,3,0:T(8,128)S(1)} %bitcast.116, f32[2,2,16,1,128,64]{4,5,2,1,3,0:T(8,128)S(1)} %bitcast.117, f32[4]{0:T(128)S(1)} %pad.4.clone, f32[2,2,16,128,64]{3,4,2,1,0:T(8,128)S(1)} %bitcast.112, ...), kind=kOutput, calls=%fused_computation.22 | convolution fusion | flops 3231711232 | bytes 17826832 | tf_op jit(solution)/shard_map/scign,sghcnp->scighp/dot_general | solution.py:113
  151.5 36.0 %fusion.21 = f32[2,4,128,2,16,64]{2,5,4,3,1,0:T(8,128)} fusion(f32[2,4,2,16,64,128]{5,4,3,2,1,0:T(8,128)S(1)} %fusion.13, f32[2,4,128,2,16]{2,4,3,1,0:T(8,128)S(1)} %get-tuple-element.16, f32[2,2,4,128,128]{4,3,1,2,0:T(8,128)S(1)} %fusion.55, f32[2,2,16,4,128]{4,2,1,3,0:T(8,128)S(1)} %get-tuple-element.14, f32[2,2,16,4,128]{4,2,1,3,0:T(8,128)S(1)} %bitcast.120, ...), kind=kOutput, calls=%fused_computation.33 | convolution fusion | flops 3242196992 | bytes 26624000 | tf_op jit(solution)/shard_map/sghcij,scjghp->scighp/dot_general | solution.py:73
  187.5 14.6 %copy.81 = f32[2,4,128,2,16,64]{2,1,5,4,3,0:T(4,128)} copy(f32[2,4,128,2,16,64]{2,5,4,3,1,0:T(8,128)} %fusion.21) | data formatting | bytes 16777216 | tf_op jit(solution)/shard_map/add | solution.py:116
  202.1 10.8 %reshape.151 = f32[2,512,2048]{1,2,0:T(8,128)} reshape(f32[2,4,128,2,16,64]{2,1,5,4,3,0:T(4,128)} %copy.81) | data formatting | bytes 16777216 | tf_op jit(solution)/shard_map/reshape | solution.py:116
  212.9 6.2 bitcast_reduce_fusion
  219.1 1.0 copy-done
  220.1 1.2 copy-done.2
  221.3 4.2 fusion.20
  225.5 6.6 %copy.83 = bf16[2,512,2048]{2,1,0:T(8,128)(2,1)} copy(bf16[2,512,2048]{1,2,0:T(8,128)(2,1)} %fusion.20) | data formatting | bytes 8388608 | tf_op jit(solution)/shard_map/convert_element_type | solution.py:120
  232.1 67.3 %all-gather.7.cloned.1.call-done = bf16[2048,8192]{1,0:T(8,128)(2,1)} async-done(((bf16[2048,1024]{1,0:T(8,128)(2,1)}), bf16[2048,8192]{1,0:T(8,128)(2,1)}) %all-gather.7.cloned.1.call-update) | async-done | bytes 33554448 | tf_op jit(solution)/shard_map/all_gather | solution.py:124
  299.4 41.9 %convolution_convert_fusion = bf16[1024,8192]{1,0:T(8,128)(2,1)} fusion(bf16[1024,2048]{1,0:T(8,128)(2,1)} %bitcast.118, bf16[2048,8192]{1,0:T(8,128)(2,1)} %all-gather.7.cloned.1.call-done), kind=kOutput, calls=%fused_computation.7 | convolution fusion | flops 34368126976 | bytes 54525952 | tf_op jit(solution)/shard_map/dot_general | solution.py:122
  341.3 280.5 %reduce-scatter.2.cloned.1.call-done = bf16[1024,2048]{1,0:T(8,128)(2,1)} async-done(((bf16[1024,8192]{1,0:T(8,128)(2,1)}), bf16[1024,2048]{1,0:T(8,128)(2,1)}) %reduce-scatter.2.cloned.1.call-update) | async-done | bytes 4194320 | tf_op jit(solution)/shard_map/reduce_scatter | solution.py:127
  (71 shorter events, 10.1 us)
Async XLA Ops:
  6.5 21.3 %copy-start.6 = (bf16[2,512,256]{2,1,0:T(8,128)(2,1)S(1)}, bf16[2,512,256]{2,1,0:T(8,128)(2,1)}, u32[]{:S(2)}) copy-start(bf16[2,512,256]{2,1,0:T(8,128)(2,1)} %param.13) | copy-start | bytes 1572868
  6.5 130.1 %all-gather.5.cloned.1.call-start = ((), (), s32[]{:S(2)}) async-start(), calls=%async_computation.1 | async-start | bytes 9437184 | tf_op jit(solution)/shard_map/all_gather | solution.py:95
  7.5 21.6 %collective-permute-start = (bf16[2,3,2048]{2,0,1:T(2,128)(2,1)S(1)}, bf16[2,3,2048]{2,0,1:T(2,128)(2,1)S(1)}, u32[]{:S(2)}, u32[]{:S(2)}) collective-permute-start(bf16[2,3,2048]{2,0,1:T(2,128)(2,1)S(1)} %copy.90), channel_id=1, source_target_pairs={{0,4},{4,8},{8,12},{12,16},{16,20},{20,24},{24,28},{1,5},{5,9},{9,... | collective-permute-start | bytes 73736 | tf_op jit(solution)/shard_map/ppermute | solution.py:18
  10.6 17.2 %collective-permute-start.2 = (bf16[2,3,256]{2,1,0:T(4,128)(2,1)S(1)}, bf16[2,3,256]{2,1,0:T(4,128)(2,1)S(1)}, u32[]{:S(2)}, u32[]{:S(2)}) collective-permute-start(bf16[2,3,256]{2,1,0:T(4,128)(2,1)S(1)} %slice.131), channel_id=1, source_target_pairs={{0,4},{4,8},{8,12},{12,16},{16,20},{20,24},{24,28},{1,5},{5,9},{9,... | collective-permute-start | bytes 9224 | tf_op jit(solution)/shard_map/ppermute | solution.py:18
  20.5 56.4 %copy-start.10 = (f32[2,32,1]{1,2,0:T(1,128)}, f32[2,32,1]{1,2,0:T(1,128)S(1)}, u32[]{:S(2)}) copy-start(f32[2,32,1]{1,2,0:T(1,128)S(1)} %get-tuple-element.31) | copy-start | bytes 772
  20.5 56.4 %copy-start.11 = (f32[2,32,1]{1,2,0:T(1,128)}, f32[2,32,1]{1,2,0:T(1,128)S(1)}, u32[]{:S(2)}) copy-start(f32[2,32,1]{1,2,0:T(1,128)S(1)} %get-tuple-element.32) | copy-start | bytes 772
  76.8 3.2 copy-start.1
  76.8 5.8 copy-start.7
  76.9 16.7 %copy-start.13 = (f32[4,256]{1,0:T(4,128)S(1)}, f32[4,256]{1,0:T(4,128)}, u32[]{:S(2)}) copy-start(f32[4,256]{1,0:T(4,128)} %param.19) | copy-start | bytes 12292
  81.8 217.6 %all-gather.7.cloned.1.call-start = ((), (), s32[]{:S(2)}) async-start(), calls=%async_computation.2 | async-start | bytes 37748736 | tf_op jit(solution)/shard_map/all_gather | solution.py:124
  82.6 539.2 %reduce-scatter.2.cloned.1.call-start = ((), (), s32[]{:S(2)}) async-start(), calls=%async_computation.3 | async-start | bytes 20971520 | tf_op jit(solution)/shard_map/reduce_scatter | solution.py:127
  82.6 18.9 %collective-permute-start.1 = (bf16[2,3,256]{2,1,0:T(4,128)(2,1)S(1)}, bf16[2,3,256]{2,1,0:T(4,128)(2,1)S(1)}, u32[]{:S(2)}, u32[]{:S(2)}) collective-permute-start(bf16[2,3,256]{2,1,0:T(4,128)(2,1)S(1)} %slice.122), channel_id=1, source_target_pairs={{0,4},{4,8},{8,12},{12,16},{16,20},{20,24},{24,28},{1,5},{5,9},{9,... | collective-permute-start | bytes 9224 | tf_op jit(solution)/shard_map/ppermute | solution.py:18
  105.2 31.5 %copy-start.8 = (f32[8,2,32]{2,1,0:T(2,128)S(1)}, f32[8,2,32]{2,1,0:T(2,128)}, u32[]{:S(2)}) copy-start(f32[8,2,32]{2,1,0:T(2,128)} %select_exponential_fusion) | copy-start | bytes 6148
  136.7 5.4 copy-start.3
  136.7 5.4 copy-start.4
  136.7 5.4 copy-start.5
  136.7 14.8 %slice-start = ((s8[8388608]{0:T(1024)(128)(4,1)}), s8[4194304]{0:T(1024)(128)(4,1)S(1)}, s32[]{:S(2)}) async-start(s8[8388608]{0:T(1024)(128)(4,1)} %bitcast.110), calls=%async_computation.4 | async-start | bytes 8388608
  142.1 9.4 %slice-start.1 = ((s8[8388608]{0:T(1024)(128)(4,1)}), s8[4194304]{0:T(1024)(128)(4,1)S(1)}, s32[]{:S(2)}) async-start(s8[8388608]{0:T(1024)(128)(4,1)} %bitcast.110), calls=%async_computation.5 | async-start | bytes 8388608
  142.1 9.4 %copy-start.9 = (pred[128,128]{1,0:T(8,128)(4,1)S(1)}, pred[128,128]{1,0:T(8,128)(4,1)}, u32[]{:S(2)}) copy-start(pred[128,128]{1,0:T(8,128)(4,1)} %iota_compare_fusion) | copy-start | bytes 49156
  212.9 7.2 %copy-start = (f32[2,512,2048]{1,2,0:T(8,128)S(1)}, f32[2,512,2048]{1,2,0:T(8,128)}, u32[]{:S(2)}) copy-start(f32[2,512,2048]{1,2,0:T(8,128)} %reshape.151) | copy-start | bytes 25165828
  212.9 8.4 %copy-start.2 = (bf16[2,512,2048]{1,2,0:T(8,128)(2,1)S(1)}, bf16[2,512,2048]{1,2,0:T(8,128)(2,1)}, u32[]{:S(2)}) copy-start(bf16[2,512,2048]{1,2,0:T(8,128)(2,1)} %copy.82) | copy-start | bytes 12582916
  212.9 8.4 %copy-start.12 = (f32[2048]{0:T(1024)S(1)}, f32[2048]{0:T(1024)}, u32[]{:S(2)}) copy-start(f32[2048]{0:T(1024)} %param.20) | copy-start | bytes 24580
Sparse Core Ops, SparseCore 0:
  81.9 54.7 all-gather.4
  138.6 160.7 all-gather.6
  341.4 280.2 reduce-scatter.1
where the time goes:
time: 637 us; the launch traced here: 629 us
  waiting for transfers between devices  373 us (59%)
  matrix products  101 us (16%)
  local copies, waits for them, and re-layouts  67.5 us (11%)
  other arithmetic  55.6 us (9%)
  between operations  13.9 us (2%)
  blocking collectives  8.9 us (1%)
  starting transfers between devices  8.86 us (1%)
    reduce_scatter x1, waiting for transfers between devices, per_device(): lax.psum_scatter(partial_out.astype(jnp.bfloat16), 'head', scatter_dimens...  280 us
    all_gather x1, waiting for transfers between devices, per_device(): lax.all_gather(out_weight, 'seq', axis=1, tiled=True)  67.3 us
    dot_general x1, matrix products, per_device(): jnp.dot(token_rows, lax.all_gather(out_weight, 'seq', axis=1, tiled=True)...  41.9 us
    dot_general x1, matrix products, per_device(): jnp.einsum('sghcij,scjghp->scighp', mixing, values_blocks, precision=HIGH)  36 us
    all_gather x1, waiting for transfers between devices, per_device(): lax.all_gather(final_state[None].astype(jnp.bfloat16), 'seq', axis=0, til...  24.9 us
    unnamed x35, local copies, waits for them, and re-layouts  18.3 us
    add x1, local copies, waits for them, and re-layouts, per_device(): ssd_out = (diagonal + reading).reshape(seqs, length, width)  14.6 us
  transfers between devices with their start and end apart: 6, of which 3 were waited for; matrix products, arithmetic and copies ran while one was open for 20% of the time, Pallas kernels for 0%

commit v1 on v0

v1 whole, which is shorter than its diff:
```python
import functools

import jax
import jax.numpy as jnp
from jax import lax
from jax.experimental import pallas as pl
from jax.experimental.pallas import tpu as pltpu
from jax.sharding import PartitionSpec as P

HEAD_DIM = 64
STATE = 128
CONV = 4
SPAN = 128
RIM = 16
ROWS = 64
COLS = 256
F32 = jnp.float32
BF16 = jnp.bfloat16


def shifted(value, axis, steps):
    count = lax.axis_size(axis)
    initial, last = (max(0, -steps), min(count, count - steps))
    return lax.ppermute(value, axis, [(source, source + steps) for source in range(initial, last)])


def conv_into(out_ref, in_ref, rim_ref, taps_ref):
    length, width = in_ref.shape[1:]
    cols = min(COLS, width)
    for c in range(0, width, cols):
        taps = taps_ref[:, c : c + cols]
        for r in range(0, length, ROWS):
            if r == 0:
                tile = jnp.concatenate(
                    [rim_ref[0, :, c : c + cols], in_ref[0, 0:ROWS, c : c + cols]], axis=0
                )
            else:
                tile = in_ref[0, r - RIM : r + ROWS, c : c + cols]
            tile = tile.astype(F32)
            total = taps[CONV - 1 : CONV] * tile[RIM:]
            for tap in range(CONV - 1):
                start = RIM - (CONV - 1) + tap
                total = total + taps[tap : tap + 1] * tile[start : start + ROWS]
            total = total / (1.0 + jnp.exp(-total))
            out_ref[0, r : r + ROWS, c : c + cols] = total.astype(out_ref.dtype)


def local_kernel(
    x_ref, w_ref, r_ref, xr_ref, wr_ref, rr_ref, xt_ref, wt_ref, rt_ref, win_ref, exp_ref,
    v_out, w_out, r_out, s_out,
):
    conv_into(w_out, w_ref, wr_ref, wt_ref)
    conv_into(r_out, r_ref, rr_ref, rt_ref)
    conv_into(v_out, x_ref, xr_ref, xt_ref)
    length = v_out.shape[1]
    total = None
    for r in range(0, length, SPAN):
        spread = jnp.dot(win_ref[0, 0, r : r + SPAN, :], exp_ref[...], preferred_element_type=F32)
        scaled = (v_out[0, r : r + SPAN, :].astype(F32) * spread).astype(BF16)
        part = lax.dot_general(
            w_out[0, r : r + SPAN, :], scaled, (((0,), (0,)), ((), ())), preferred_element_type=F32
        )
        total = part if total is None else total + part
    s_out[0] = total.astype(s_out.dtype)


def scan_kernel(
    per_group, v_ref, w_ref, r_ref, gate_ref, ct_ref, cr_ref, st_ref, et_ref, wn_ref, dec_ref,
    carry_ref, gain_ref, exp_ref, out_ref, state_ref,
):
    @pl.when(pl.program_id(2) == 0)
    def _():
        state_ref[...] = carry_ref[0]

    writes, reads = w_ref[0], r_ref[0]
    scores = lax.dot_general(reads, writes, (((1,), (1,)), ((), ())), preferred_element_type=F32)
    rows = lax.broadcasted_iota(jnp.int32, (SPAN, SPAN), 0)
    cols = lax.broadcasted_iota(jnp.int32, (SPAN, SPAN), 1)
    later = rows >= cols
    scores = jnp.where(later, scores, 0.0)
    values = v_ref[0]
    spread = jnp.dot(et_ref[0, 0], exp_ref[...], preferred_element_type=F32)
    reading = jnp.dot(reads, state_ref[...].astype(BF16), preferred_element_type=F32) * spread
    half = lax.broadcasted_iota(jnp.int32, (SPAN, 2 * HEAD_DIM), 1) < HEAD_DIM
    squares = jnp.zeros((SPAN, 1), F32)
    parts = []
    for pair in range(per_group // 2):
        mixes = []
        for head in (2 * pair, 2 * pair + 1):
            gap = ct_ref[0, 0, :, head : head + 1] - cr_ref[0, 0, head : head + 1, :]
            gap = jnp.where(later, gap, 0.0)
            mixes.append((jnp.exp(gap) * st_ref[0, 0, head : head + 1, :] * scores).astype(BF16))
        at = slice(pair * 2 * HEAD_DIM, (pair + 1) * 2 * HEAD_DIM)
        both = values[:, at]
        zero = jnp.zeros_like(both)
        stacked = jnp.concatenate([jnp.where(half, both, zero), jnp.where(half, zero, both)], axis=0)
        ssd = jnp.dot(jnp.concatenate(mixes, axis=1), stacked, preferred_element_type=F32)
        ssd = ssd + reading[:, at]
        gate = gate_ref[0, :, at].astype(F32)
        gated = ssd * (gate / (1.0 + jnp.exp(-gate)))
        squares = squares + jnp.sum(gated * gated, axis=1, keepdims=True)
        parts.append(gated)
    scale = lax.rsqrt(squares / (per_group * HEAD_DIM) + 1e-05)
    for pair in range(per_group // 2):
        at = slice(pair * 2 * HEAD_DIM, (pair + 1) * 2 * HEAD_DIM)
        out_ref[0, :, at] = (parts[pair] * scale * gain_ref[:, at]).astype(BF16)

    @pl.when(pl.program_id(2) < pl.num_programs(2) - 1)
    def _():
        weight = jnp.dot(wn_ref[0, 0], exp_ref[...], preferred_element_type=F32)
        scaled = (values.astype(F32) * weight).astype(BF16)
        fresh = lax.dot_general(
            writes, scaled, (((0,), (0,)), ((), ())), preferred_element_type=F32
        )
        state_ref[...] = state_ref[...] * dec_ref[0, 0] + fresh


def project(normed, out_weight, n_head):
    seqs, length, _ = normed.shape
    gathered = lax.all_gather(out_weight, "seq", axis=0)
    pieces = gathered.shape[0] // n_head
    me = lax.axis_index("head")

    def partial(rows, block):
        block = jnp.clip(block, 0, n_head - 1)
        cut = lax.dynamic_slice_in_dim(gathered, block * pieces, pieces, 0)
        return jnp.concatenate(
            [jnp.dot(rows, cut[p], preferred_element_type=F32) for p in range(pieces)], axis=1
        )

    sums = [[None, None] for _ in range(seqs)]
    for slot in range(1, n_head):
        for s in range(seqs):
            for way, sign in ((0, 1), (1, -1)):
                term = partial(normed[s], me + sign * (n_head - slot))
                if sums[s][way] is not None:
                    term = term + sums[s][way].astype(F32)
                if sign > 0:
                    pairs = [(z, z + 1) for z in range(slot)]
                else:
                    pairs = [(n_head - 1 - z, n_head - 2 - z) for z in range(slot)]
                sums[s][way] = lax.ppermute(term.astype(BF16), "head", pairs)
    outs = [
        (partial(normed[s], me) + sums[s][0].astype(F32) + sums[s][1].astype(F32)).astype(BF16)
        for s in range(seqs)
    ]
    return jnp.stack(outs, axis=0)


def per_device(
    n_head,
    head_inputs,
    gate_inputs,
    state_writes,
    state_reads,
    step_raw,
    decay_log,
    conv_inputs,
    conv_writes,
    conv_reads,
    norm_gain,
    out_weight,
):
    seqs, length, width = head_inputs.shape
    heads = decay_log.shape[0]
    groups = state_writes.shape[2] // STATE
    per_group = heads // groups
    gw = width // groups
    spans = length // SPAN
    rims = shifted(
        (
            head_inputs[:, length - RIM :],
            state_writes[:, length - RIM :],
            state_reads[:, length - RIM :],
        ),
        "seq",
        1,
    )
    steps = jax.nn.softplus(step_raw)
    log_decay = steps * (-jnp.exp(decay_log))[None, :, None]
    steps_blocks = steps.reshape(seqs, heads, spans, SPAN)
    cumul = jnp.cumsum(log_decay.reshape(seqs, heads, spans, SPAN), axis=-1)
    ends = cumul[..., -1]
    after = jnp.flip(jnp.cumsum(jnp.flip(ends, -1), -1), -1) - ends

    def by_time(x):
        x = x.reshape(seqs, groups, per_group, length)
        return x.transpose(0, 1, 3, 2)

    def by_head(x):
        x = x.reshape(seqs, groups, per_group, spans, SPAN).transpose(0, 1, 3, 2, 4)
        return x.reshape(seqs, groups * spans, per_group, SPAN)

    ct = by_time(cumul)
    et = by_time(jnp.exp(cumul)).astype(BF16)
    win = jnp.exp(ends[..., None] - cumul) * steps_blocks
    wn = by_time(win).astype(BF16)
    wfar = by_time(jnp.exp(after[..., None] + ends[..., None] - cumul) * steps_blocks).astype(BF16)
    cr, st = by_head(cumul), by_head(steps_blocks)
    dec = jnp.repeat(jnp.exp(ends).transpose(0, 2, 1), HEAD_DIM, axis=2)[:, :, None, :]
    expand = (jnp.arange(per_group)[:, None] == jnp.arange(gw)[None, :] // HEAD_DIM).astype(BF16)

    def spec(shape, index):
        return pl.BlockSpec(shape, index)

    tall = lambda w: spec((1, length, w), lambda s, g: (s, 0, g))
    edge = lambda w: spec((1, RIM, w), lambda s, g: (s, 0, g))
    tap = lambda w: spec((CONV, w), lambda s, g: (0, g))
    values, writes, reads, finals = pl.pallas_call(
        local_kernel,
        grid=(seqs, groups),
        in_specs=[
            tall(gw), tall(STATE), tall(STATE), edge(gw), edge(STATE), edge(STATE),
            tap(gw), tap(STATE), tap(STATE),
            spec((1, 1, length, per_group), lambda s, g: (s, g, 0, 0)),
            spec((per_group, gw), lambda s, g: (0, 0)),
        ],
        out_specs=[
            tall(gw), tall(STATE), tall(STATE),
            spec((1, STATE, gw), lambda s, g: (s, 0, g)),
        ],
        out_shape=[
            jax.ShapeDtypeStruct((seqs, length, width), BF16),
            jax.ShapeDtypeStruct((seqs, length, groups * STATE), BF16),
            jax.ShapeDtypeStruct((seqs, length, groups * STATE), BF16),
            jax.ShapeDtypeStruct((seqs, STATE, width), BF16),
        ],
        compiler_params=pltpu.CompilerParams(vmem_limit_bytes=48 * 2**20),
        cost_estimate=pl.CostEstimate(
            flops=4 * seqs * length * STATE * width,
            bytes_accessed=4 * seqs * length * width,
            transcendentals=seqs * length * width,
        ),
        name="local_states",
    )(head_inputs, state_writes, state_reads, *rims, conv_inputs, conv_writes, conv_reads, wfar, expand)

    device_logs = jnp.sum(ends, axis=-1)
    all_logs = lax.all_gather(device_logs[None], "seq", axis=0, tiled=True)
    before = jnp.cumsum(all_logs, axis=0) - all_logs
    own = lax.axis_index("seq")
    own_before = lax.dynamic_index_in_dim(before, own, 0, keepdims=False)
    pieces = lax.all_gather(finals, "seq", axis=0)
    source = jnp.arange(pieces.shape[0], dtype=jnp.int32)
    far = jnp.where((source < own)[:, None, None], own_before[None] - before - all_logs, -jnp.inf)
    far = jnp.repeat(jnp.exp(far), HEAD_DIM, axis=2)
    carried = jnp.sum(far[:, :, None, :] * pieces.astype(F32), axis=0)

    block = lambda w: spec((1, SPAN, w), lambda s, g, c: (s, c, g))
    timed = spec((1, 1, SPAN, per_group), lambda s, g, c: (s, g, c, 0))
    headed = spec((1, 1, per_group, SPAN), lambda s, g, c: (s, g * spans + c, 0, 0))
    normed = pl.pallas_call(
        functools.partial(scan_kernel, per_group),
        grid=(seqs, groups, spans),
        in_specs=[
            block(gw), block(STATE), block(STATE), block(gw),
            timed, headed, headed, timed, timed,
            spec((1, 1, 1, gw), lambda s, g, c: (s, c, 0, g)),
            spec((1, STATE, gw), lambda s, g, c: (s, 0, g)),
            spec((1, gw), lambda s, g, c: (0, g)),
            spec((per_group, gw), lambda s, g, c: (0, 0)),
        ],
        out_specs=block(gw),
        out_shape=jax.ShapeDtypeStruct((seqs, length, width), BF16),
        scratch_shapes=[pltpu.VMEM((STATE, gw), F32)],
        compiler_params=pltpu.CompilerParams(vmem_limit_bytes=48 * 2**20),
        cost_estimate=pl.CostEstimate(
            flops=8 * seqs * length * STATE * width,
            bytes_accessed=6 * seqs * length * width,
            transcendentals=4 * seqs * length * width,
        ),
        name="span_scan",
    )(values, writes, reads, gate_inputs, ct, cr, st, et, wn, dec, carried, norm_gain[None], expand)
    return project(normed, out_weight, n_head)


def solution(mesh):
    return jax.shard_map(
        functools.partial(per_device, mesh.shape["head"]),
        mesh=mesh,
        in_specs=(
            P(None, "seq", "head"),
            P(None, "seq", "head"),
            P(None, "seq", "head"),
            P(None, "seq", "head"),
            P(None, "head", "seq"),
            P("head"),
            P(None, "head"),
            P(None, "head"),
            P(None, "head"),
            P("head"),
            P("head", "seq"),
        ),
        out_specs=P(None, "seq", "head"),
        check_vma=False,
    )
```

time: 637 us -> 646 us (1.014)
  local copies, waits for them, and re-layouts: 67.5 us -> 10.7 us
  Pallas kernels: 0 us -> 39.7 us
  starting transfers between devices: 8.86 us -> 45.9 us
  matrix products: 101 us -> 138 us
  waiting for transfers between devices: 373 us -> 337 us
  other arithmetic: 55.6 us -> 40.9 us
    reduce_scatter x1 -> x0, waiting for transfers between devices: 280 us -> none  [per_device(): lax.psum_scatter(partial_out.astype(jnp.bfloat16), 'head', scatter_dimens...]
    ppermute x0 -> x12, waiting for transfers between devices: none -> 163 us  [project(): sums[s][way] = lax.ppermute(term.astype(BF16), 'head', pairs)]
    all_gather x2, waiting for transfers between devices: 92.1 us -> 173 us  [the longest x1 131 us: project(): gathered = lax.all_gather(out_weight, 'seq', axis=0)]
    pallas_call x0 -> x2, Pallas kernels: none -> 39.7 us  [the longest x1 26.6 us: per_device(): pl.pallas_call(functools.partial(scan_kernel, per_group), grid=(seqs, gro...]
    ppermute x0 -> x12, starting transfers between devices: none -> 37.1 us  [project(): sums[s][way] = lax.ppermute(term.astype(BF16), 'head', pairs)]
    dot_general x5 -> x28, matrix products: 101 us -> 138 us  [partial(): jnp.dot(rows, cut[p], preferred_element_type=F32)]
    reshape x4 -> x2, local copies, waits for them, and re-layouts: 21.8 us -> 1.34 us  [the longest x1 1.33 us: per_device(): steps_blocks = steps.reshape(seqs, heads, spans, SPAN)]
    unnamed x35 -> x22, local copies, waits for them, and re-layouts: 18.3 us -> 0.05 us
  transfers between devices with their start and end apart: 6 -> 17, of which waited for: 3 -> 8; matrix products, arithmetic and copies ran while one was open for 20% -> 15% of each run, Pallas kernels for 0% -> 4%
where the time goes in v1:
time: 646 us; the launch traced here: 636 us
  waiting for transfers between devices  337 us (52%)
  matrix products  138 us (21%)
  starting transfers between devices  45.9 us (7%)
  other arithmetic  40.9 us (6%)
  Pallas kernels  39.7 us (6%)
  between operations  14.6 us (2%)
  local copies, waits for them, and re-layouts  10.7 us (2%)
  blocking collectives  8.89 us (1%)
    ppermute x12, waiting for transfers between devices, project(): sums[s][way] = lax.ppermute(term.astype(BF16), 'head', pairs)  163 us
    dot_general x28, matrix products, partial(): jnp.dot(rows, cut[p], preferred_element_type=F32)  138 us
    all_gather x1, waiting for transfers between devices, project(): gathered = lax.all_gather(out_weight, 'seq', axis=0)  131 us
    all_gather x1, waiting for transfers between devices, per_device(): pieces = lax.all_gather(finals, 'seq', axis=0)  42.9 us
    ppermute x12, starting transfers between devices, project(): sums[s][way] = lax.ppermute(term.astype(BF16), 'head', pairs)  37.1 us
    pallas_call x1, Pallas kernels, per_device(): pl.pallas_call(functools.partial(scan_kernel, per_group), grid=(seqs, gro...  26.6 us
    convert_element_type x8, other arithmetic, project(): sums[s][way] = lax.ppermute(term.astype(BF16), 'head', pairs)  23.8 us
    pallas_call x1, Pallas kernels, per_device(): pl.pallas_call(local_kernel, grid=(seqs, groups), in_specs=[tall(gw), tal...  13.1 us
  transfers between devices with their start and end apart: 17, of which 8 were waited for; matrix products, arithmetic and copies ran while one was open for 15% of the time, Pallas kernels for 4%

profile of v1, /device:TPU:0, one launch (start us, length us, event | category | flops | bytes accessed | tf_op | source)
XLA Modules:
  0.0 635.8 jit_solution(2913176440571028332)
XLA Ops:
  29.0 13.1 %local_states.1 = (bf16[2,512,2048]{2,1,0:T(8,128)(2,1)}, bf16[2,512,256]{2,1,0:T(8,128)(2,1)S(1)}, bf16[2,512,256]{2,1,0:T(8,128)(2,1)S(1)}, bf16[2,128,2048]{2,1,0:T(8,128)(2,1)}) custom-call(bf16[2,512,2048]{2,1,0:T(8,128)(2,1)} %x_ref.1, bf16[2,512,256]{2,1,0:T(8,128)(2,1)S(1)} %copy-done, bf16[2,512,256]{2,1,0:T(8,128)(2,1)S(1)} %copy-done.1, ...), custom_call_target="tpu_custom_call" | custom-call | flops 1073741824 | bytes 8388608 | tf_op jit(solution)/shard_map/local_states/pallas_call | solution.py:209
  43.9 8.9 %all-gather.3 = f32[8,2,32]{2,1,0:T(2,128)S(1)} all-gather(f32[1,2,32]{2,1,0:T(2,128)S(1)} %bitcast.154), channel_id=2, replica_groups=mesh['seq'=8,'head'=4] {'seq'}, dimensions={0}, use_global_device_ids=true | all-gather | bytes 2304 | tf_op jit(solution)/shard_map/all_gather | solution.py:238
  55.3 42.9 %all-gather.7.cloned.1.call-done = bf16[16,128,2048]{2,1,0:T(8,128)(2,1)} async-done(((bf16[2,128,2048]{2,1,0:T(8,128)(2,1)}), bf16[16,128,2048]{2,1,0:T(8,128)(2,1)}) %all-gather.7.cloned.1.call-update) | async-done | bytes 8388624 | tf_op jit(solution)/shard_map/all_gather | solution.py:242
  98.2 5.6 fusion.carry_ref
  103.8 26.6 %span_scan.1 = bf16[2,512,2048]{2,1,0:T(8,128)(2,1)} custom-call(bf16[2,512,2048]{2,1,0:T(8,128)(2,1)} %get-tuple-element.9.v_ref, bf16[2,512,256]{2,1,0:T(8,128)(2,1)S(1)} %get-tuple-element.10.w_ref, bf16[2,512,256]{2,1,0:T(8,128)(2,1)S(1)} %get-tuple-element.11.r_ref, bf16[2,512,2048]{2,1,0:T(8,128)(2,1)} %gate_ref.1, f32[2,2,512,16]{3,2,1,0:T(8,128)S(1)} %bitcast.144, ...), custom_call_target="tpu_custom_call" | custom-call | flops 2147483648 | bytes 12582912 | tf_op jit(solution)/shard_map/span_scan/pallas_call | solution.py:251
  130.4 130.5 %all-gather.9.cloned.1.call-done = bf16[16384,1024]{1,0:T(8,128)(2,1)} async-done(((bf16[2048,1024]{1,0:T(8,128)(2,1)}), bf16[16384,1024]{1,0:T(8,128)(2,1)}) %all-gather.9.cloned.1.call-update) | async-done | bytes 33554448 | tf_op jit(solution)/shard_map/all_gather | solution.py:120
  260.9 5.3 fusion.49
  266.2 5.9 fusion.22
  276.6 4.5 fusion.45
  294.8 5.0 fusion.47
  299.8 4.5 fusion.48
  308.9 5.9 fusion.24
  328.4 4.7 fusion.19
  337.6 4.5 fusion.43
  342.2 4.5 fusion.44
  346.8 4.5 fusion.46
  351.5 4.8 collective-permute-start.3
  358.5 5.8 fusion.36
  369.5 5.9 fusion.35
  375.4 5.9 fusion.33
  385.8 5.9 fusion.32
  391.7 9.2 %collective-permute-done.3 = bf16[512,2048]{1,0:T(8,128)(2,1)} collective-permute-done((bf16[512,2048]{1,0:T(8,128)(2,1)S(1)}, bf16[512,2048]{1,0:T(8,128)(2,1)}, u32[]{:S(2)}, u32[]{:S(2)}) %collective-permute-start.3) | collective-permute-done | bytes 2097184 | tf_op jit(solution)/shard_map/ppermute | solution.py:142
  400.8 4.9 fusion.4
  405.8 5.8 collective-permute-start.4
  418.0 27.8 %collective-permute-done.9 = bf16[512,2048]{1,0:T(8,128)(2,1)} collective-permute-done((bf16[512,2048]{1,0:T(8,128)(2,1)S(1)}, bf16[512,2048]{1,0:T(8,128)(2,1)}, u32[]{:S(2)}, u32[]{:S(2)}) %collective-permute-start.9) | collective-permute-done | bytes 2097184 | tf_op jit(solution)/shard_map/ppermute | solution.py:142
  449.4 4.6 collective-permute-start.10
  457.4 5.9 fusion.31
  463.3 27.6 %collective-permute-done.4 = bf16[512,2048]{1,0:T(8,128)(2,1)} collective-permute-done((bf16[512,2048]{1,0:T(8,128)(2,1)}, bf16[512,2048]{1,0:T(8,128)(2,1)}, u32[]{:S(2)}, u32[]{:S(2)}) %collective-permute-start.4) | collective-permute-done | bytes 2097184 | tf_op jit(solution)/shard_map/ppermute | solution.py:142
  502.7 33.1 %collective-permute-done.10 = bf16[512,2048]{1,0:T(8,128)(2,1)S(1)} collective-permute-done((bf16[512,2048]{1,0:T(8,128)(2,1)}, bf16[512,2048]{1,0:T(8,128)(2,1)S(1)}, u32[]{:S(2)}, u32[]{:S(2)}) %collective-permute-start.10) | collective-permute-done | bytes 2097184 | tf_op jit(solution)/shard_map/ppermute | solution.py:142
  544.6 4.5 fusion.16
  558.3 22.4 %collective-permute-done.5 = bf16[512,2048]{1,0:T(8,128)(2,1)S(1)} collective-permute-done((bf16[512,2048]{1,0:T(8,128)(2,1)S(1)}, bf16[512,2048]{1,0:T(8,128)(2,1)S(1)}, u32[]{:S(2)}, u32[]{:S(2)}) %collective-permute-start.5) | collective-permute-done | bytes 2097184 | tf_op jit(solution)/shard_map/ppermute | solution.py:142
  581.7 43.3 %collective-permute-done.11 = bf16[512,2048]{1,0:T(8,128)(2,1)S(1)} collective-permute-done((bf16[512,2048]{1,0:T(8,128)(2,1)}, bf16[512,2048]{1,0:T(8,128)(2,1)S(1)}, u32[]{:S(2)}, u32[]{:S(2)}) %collective-permute-start.11) | collective-permute-done | bytes 2097184 | tf_op jit(solution)/shard_map/ppermute | solution.py:142
  (115 shorter events, 127.1 us)
Async XLA Ops:
  6.5 91.7 %all-gather.7.cloned.1.call-start = ((), (), s32[]{:S(2)}) async-start(), calls=%async_computation | async-start | bytes 9437184 | tf_op jit(solution)/shard_map/all_gather | solution.py:242
  8.1 20.8 %collective-permute-start = (bf16[2,16,2048]{2,1,0:T(8,128)(2,1)}, bf16[2,16,2048]{2,1,0:T(8,128)(2,1)S(1)}, u32[]{:S(2)}, u32[]{:S(2)}) collective-permute-start(bf16[2,16,2048]{2,1,0:T(8,128)(2,1)} %slice.40), channel_id=1, source_target_pairs={{0,4},{4,8},{8,12},{12,16},{16,20},{20,24},{24,28},{1,5},{5,9},{9,... | collective-permute-start | bytes 393224 | tf_op jit(solution)/shard_map/ppermute | solution.py:24
  11.2 17.7 %collective-permute-start.1 = (bf16[2,16,256]{2,1,0:T(8,128)(2,1)S(1)}, bf16[2,16,256]{2,1,0:T(8,128)(2,1)S(1)}, u32[]{:S(2)}, u32[]{:S(2)}) collective-permute-start(bf16[2,16,256]{2,1,0:T(8,128)(2,1)S(1)} %slice.41), channel_id=1, source_target_pairs={{0,4},{4,8},{8,12},{12,16},{16,20},{20,24},{24,28},{1,5},{5,9},{9,... | collective-permute-start | bytes 49160 | tf_op jit(solution)/shard_map/ppermute | solution.py:24
  16.4 12.5 %collective-permute-start.2 = (bf16[2,16,256]{2,1,0:T(8,128)(2,1)S(1)}, bf16[2,16,256]{2,1,0:T(8,128)(2,1)S(1)}, u32[]{:S(2)}, u32[]{:S(2)}) collective-permute-start(bf16[2,16,256]{2,1,0:T(8,128)(2,1)S(1)} %slice.42), channel_id=1, source_target_pairs={{0,4},{4,8},{8,12},{12,16},{16,20},{20,24},{24,28},{1,5},{5,9},{9,... | collective-permute-start | bytes 49160 | tf_op jit(solution)/shard_map/ppermute | solution.py:24
  24.0 4.9 copy-start
  24.1 4.9 copy-start.1
  24.1 4.9 copy-start.2
  24.1 4.9 copy-start.4
  24.1 4.9 copy-start.5
  42.1 218.8 %all-gather.9.cloned.1.call-start = ((), (), s32[]{:S(2)}) async-start(), calls=%async_computation.1 | async-start | bytes 37748736 | tf_op jit(solution)/shard_map/all_gather | solution.py:120
  98.2 5.6 copy-start.3
  260.9 5.3 copy-start.6
  351.5 49.4 %collective-permute-start.3 = (bf16[512,2048]{1,0:T(8,128)(2,1)S(1)}, bf16[512,2048]{1,0:T(8,128)(2,1)}, u32[]{:S(2)}, u32[]{:S(2)}) collective-permute-start(bf16[512,2048]{1,0:T(8,128)(2,1)S(1)} %pad_maximum_fusion.1), channel_id=1, source_target_pairs={{0,1},{4,5},{8,9},{12,13},{16,17},{20,21},{24,25},{28,29}} | collective-permute-start | bytes 6291464 | tf_op jit(solution)/shard_map/ppermute | solution.py:142
  356.5 55.1 %collective-permute-start.6 = (bf16[512,2048]{1,0:T(8,128)(2,1)S(1)}, bf16[512,2048]{1,0:T(8,128)(2,1)}, u32[]{:S(2)}, u32[]{:S(2)}) collective-permute-start(bf16[512,2048]{1,0:T(8,128)(2,1)S(1)} %pad_maximum_fusion.2), channel_id=1, source_target_pairs={{3,2},{7,6},{11,10},{15,14},{19,18},{23,22},{27,26},{31,30}} | collective-permute-start | bytes 6291464 | tf_op jit(solution)/shard_map/ppermute | solution.py:142
  364.5 81.3 %collective-permute-start.9 = (bf16[512,2048]{1,0:T(8,128)(2,1)S(1)}, bf16[512,2048]{1,0:T(8,128)(2,1)}, u32[]{:S(2)}, u32[]{:S(2)}) collective-permute-start(bf16[512,2048]{1,0:T(8,128)(2,1)S(1)} %pad_maximum_fusion.3), channel_id=1, source_target_pairs={{0,1},{4,5},{8,9},{12,13},{16,17},{20,21},{24,25},{28,29}} | collective-permute-start | bytes 6291464 | tf_op jit(solution)/shard_map/ppermute | solution.py:142
  367.3 86.7 %collective-permute-start.12 = (bf16[512,2048]{1,0:T(8,128)(2,1)S(1)}, bf16[512,2048]{1,0:T(8,128)(2,1)}, u32[]{:S(2)}, u32[]{:S(2)}) collective-permute-start(bf16[512,2048]{1,0:T(8,128)(2,1)S(1)} %pad_maximum_fusion.4), channel_id=1, source_target_pairs={{3,2},{7,6},{11,10},{15,14},{19,18},{23,22},{27,26},{31,30}} | collective-permute-start | bytes 6291464 | tf_op jit(solution)/shard_map/ppermute | solution.py:142
  405.8 85.0 %collective-permute-start.4 = (bf16[512,2048]{1,0:T(8,128)(2,1)}, bf16[512,2048]{1,0:T(8,128)(2,1)}, u32[]{:S(2)}, u32[]{:S(2)}) collective-permute-start(bf16[512,2048]{1,0:T(8,128)(2,1)} %fusion.4), channel_id=1, source_target_pairs={{0,1},{1,2},{4,5},{5,6},{8,9},{9,10},{12,13},{13,14},{16,17},{17,1... | collective-permute-start | bytes 6291464 | tf_op jit(solution)/shard_map/ppermute | solution.py:142
  415.8 38.2 %copy-start.8 = (f32[512,1024]{1,0:T(8,128)S(1)}, f32[512,1024]{1,0:T(8,128)}, u32[]{:S(2)}) copy-start(f32[512,1024]{1,0:T(8,128)} %fusion.35) | copy-start | bytes 6291460
  415.8 38.2 %copy-start.9 = (f32[512,1024]{1,0:T(8,128)S(1)}, f32[512,1024]{1,0:T(8,128)}, u32[]{:S(2)}) copy-start(f32[512,1024]{1,0:T(8,128)} %fusion.33) | copy-start | bytes 6291460
  415.8 81.8 %collective-permute-start.7 = (bf16[512,2048]{1,0:T(8,128)(2,1)}, bf16[512,2048]{1,0:T(8,128)(2,1)}, u32[]{:S(2)}, u32[]{:S(2)}) collective-permute-start(bf16[512,2048]{1,0:T(8,128)(2,1)} %fusion.6), channel_id=1, source_target_pairs={{3,2},{2,1},{7,6},{6,5},{11,10},{10,9},{15,14},{14,13},{19,18},{18... | collective-permute-start | bytes 6291464 | tf_op jit(solution)/shard_map/ppermute | solution.py:142
  449.4 86.4 %collective-permute-start.10 = (bf16[512,2048]{1,0:T(8,128)(2,1)}, bf16[512,2048]{1,0:T(8,128)(2,1)S(1)}, u32[]{:S(2)}, u32[]{:S(2)}) collective-permute-start(bf16[512,2048]{1,0:T(8,128)(2,1)} %fusion.10), channel_id=1, source_target_pairs={{0,1},{1,2},{4,5},{5,6},{8,9},{9,10},{12,13},{13,14},{16,17},{17,1... | collective-permute-start | bytes 6291464 | tf_op jit(solution)/shard_map/ppermute | solution.py:142
  456.3 86.0 %collective-permute-start.13 = (bf16[512,2048]{1,0:T(8,128)(2,1)S(1)}, bf16[512,2048]{1,0:T(8,128)(2,1)S(1)}, u32[]{:S(2)}, u32[]{:S(2)}) collective-permute-start(bf16[512,2048]{1,0:T(8,128)(2,1)S(1)} %fusion.12), channel_id=1, source_target_pairs={{3,2},{2,1},{7,6},{6,5},{11,10},{10,9},{15,14},{14,13},{19,18},{18... | collective-permute-start | bytes 6291464 | tf_op jit(solution)/shard_map/ppermute | solution.py:142
  463.3 34.4 %copy-start.7 = (f32[512,1024]{1,0:T(8,128)S(1)}, f32[512,1024]{1,0:T(8,128)}, u32[]{:S(2)}) copy-start(f32[512,1024]{1,0:T(8,128)} %fusion.32) | copy-start | bytes 6291460
  493.1 87.5 %collective-permute-start.5 = (bf16[512,2048]{1,0:T(8,128)(2,1)S(1)}, bf16[512,2048]{1,0:T(8,128)(2,1)S(1)}, u32[]{:S(2)}, u32[]{:S(2)}) collective-permute-start(bf16[512,2048]{1,0:T(8,128)(2,1)S(1)} %fusion.3), channel_id=1, source_target_pairs={{0,1},{1,2},{2,3},{4,5},{5,6},{6,7},{8,9},{9,10},{10,11},{12,13},{... | collective-permute-start | bytes 6291464 | tf_op jit(solution)/shard_map/ppermute | solution.py:142
  501.3 41.0 %copy-start.10 = (f32[512,1024]{1,0:T(8,128)S(1)}, f32[512,1024]{1,0:T(8,128)}, u32[]{:S(2)}) copy-start(f32[512,1024]{1,0:T(8,128)} %fusion.31) | copy-start | bytes 6291460
  501.3 79.4 %collective-permute-start.8 = (bf16[512,2048]{1,0:T(8,128)(2,1)}, bf16[512,2048]{1,0:T(8,128)(2,1)S(1)}, u32[]{:S(2)}, u32[]{:S(2)}) collective-permute-start(bf16[512,2048]{1,0:T(8,128)(2,1)} %fusion.5), channel_id=1, source_target_pairs={{3,2},{2,1},{1,0},{7,6},{6,5},{5,4},{11,10},{10,9},{9,8},{15,14},{... | collective-permute-start | bytes 6291464 | tf_op jit(solution)/shard_map/ppermute | solution.py:142
  537.9 87.1 %collective-permute-start.11 = (bf16[512,2048]{1,0:T(8,128)(2,1)}, bf16[512,2048]{1,0:T(8,128)(2,1)S(1)}, u32[]{:S(2)}, u32[]{:S(2)}) collective-permute-start(bf16[512,2048]{1,0:T(8,128)(2,1)} %fusion.9), channel_id=1, source_target_pairs={{0,1},{1,2},{2,3},{4,5},{5,6},{6,7},{8,9},{9,10},{10,11},{12,13},{... | collective-permute-start | bytes 6291464 | tf_op jit(solution)/shard_map/ppermute | solution.py:142
  543.0 82.0 %collective-permute-start.14 = (bf16[512,2048]{1,0:T(8,128)(2,1)S(1)}, bf16[512,2048]{1,0:T(8,128)(2,1)S(1)}, u32[]{:S(2)}, u32[]{:S(2)}) collective-permute-start(bf16[512,2048]{1,0:T(8,128)(2,1)S(1)} %fusion.11), channel_id=1, source_target_pairs={{3,2},{2,1},{1,0},{7,6},{6,5},{5,4},{11,10},{10,9},{9,8},{15,14},{... | collective-permute-start | bytes 6291464 | tf_op jit(solution)/shard_map/ppermute | solution.py:142
Sparse Core Ops, SparseCore 0:
  42.2 55.9 all-gather.6
  100.1 160.7 all-gather.8

commit v2 on v1

--- a/solution.py
+++ b/solution.py
@@ -115,36 +115,180 @@
         state_ref[...] = state_ref[...] * dec_ref[0, 0] + fresh
 
 
-def project(normed, out_weight, n_head):
-    seqs, length, _ = normed.shape
-    gathered = lax.all_gather(out_weight, "seq", axis=0)
-    pieces = gathered.shape[0] // n_head
+def chain_kernel(n, chunk, a_ref, w_ref, out_ref, buf, send_sem, recv_sem):
     me = lax.axis_index("head")
-
-    def partial(rows, block):
-        block = jnp.clip(block, 0, n_head - 1)
-        cut = lax.dynamic_slice_in_dim(gathered, block * pieces, pieces, 0)
-        return jnp.concatenate(
-            [jnp.dot(rows, cut[p], preferred_element_type=F32) for p in range(pieces)], axis=1
+    rows = a_ref.shape[0]
+    pieces, cols = w_ref.shape[0] // n, w_ref.shape[2]
+    chunks = rows // chunk
+    ways = ((0, 1), (1, -1))
+    depths = (me, n - 1 - me)
+    nexts = (lax.rem(me + 1, n), lax.rem(me + n - 1, n))
+
+    def copy(way, slot, q):
+        at = pl.ds(pl.multiple_of(q * chunk, chunk), chunk)
+        return pltpu.make_async_remote_copy(
+            src_ref=buf.at[way, slot - 1, at],
+            dst_ref=buf.at[way, slot, at],
+            send_sem=send_sem.at[way, slot - 1, q],
+            recv_sem=recv_sem.at[way, slot - 1, q],
+            device_id={"head": nexts[way]},
+            device_id_type=pl.DeviceIdType.MESH,
         )
 
-    sums = [[None, None] for _ in range(seqs)]
-    for slot in range(1, n_head):
-        for s in range(seqs):
-            for way, sign in ((0, 1), (1, -1)):
-                term = partial(normed[s], me + sign * (n_head - slot))
-                if sums[s][way] is not None:
-                    term = term + sums[s][way].astype(F32)
-                if sign > 0:
-                    pairs = [(z, z + 1) for z in range(slot)]
-                else:
-                    pairs = [(n_head - 1 - z, n_head - 2 - z) for z in range(slot)]
-                sums[s][way] = lax.ppermute(term.astype(BF16), "head", pairs)
-    outs = [
-        (partial(normed[s], me) + sums[s][0].astype(F32) + sums[s][1].astype(F32)).astype(BF16)
-        for s in range(seqs)
-    ]
-    return jnp.stack(outs, axis=0)
+    barrier = pltpu.get_barrier_semaphore()
+    for way, _ in ways:
+
+        @pl.when(depths[way] < n - 1)
+        def _():
+            pl.semaphore_signal(
+                barrier,
+                inc=1,
+                device_id={"head": nexts[way]},
+                device_id_type=pl.DeviceIdType.MESH,
+            )
+
+    outer = jnp.logical_or(me == 0, me == n - 1)
+
+    @pl.when(outer)
+    def _():
+        pl.semaphore_wait(barrier, 1)
+
+    @pl.when(jnp.logical_not(outer))
+    def _():
+        pl.semaphore_wait(barrier, 2)
+
+    def send(index, carry):
+        slot, q = index // chunks + 1, index % chunks
+        at = pl.ds(pl.multiple_of(q * chunk, chunk), chunk)
+        for way, sign in ways:
+
+            @pl.when(depths[way] < slot)
+            def _():
+                block = me + sign * (n - slot)
+
+                @pl.when(depths[way] == 0)
+                def _():
+                    buf[way, slot - 1, at, :] = jnp.zeros((chunk, pieces * cols), BF16)
+
+                @pl.when(depths[way] > 0)
+                def _():
+                    copy(way, slot - 1, q).wait_recv()
+
+                for p in range(pieces):
+                    term = jnp.dot(a_ref[at, :], w_ref[block * pieces + p], preferred_element_type=F32)
+                    lanes = slice(p * cols, (p + 1) * cols)
+                    term = term + buf[way, slot - 1, at, lanes].astype(F32)
+                    buf[way, slot - 1, at, lanes] = term.astype(BF16)
+                copy(way, slot, q).start()
+
+        return carry
+
+    lax.fori_loop(0, (n - 1) * chunks, send, 0)
+
+    def finish(q, carry):
+        at = pl.ds(pl.multiple_of(q * chunk, chunk), chunk)
+        for way, _ in ways:
+
+            @pl.when(depths[way] == 0)
+            def _():
+                buf[way, n - 1, at, :] = jnp.zeros((chunk, pieces * cols), BF16)
+
+            @pl.when(depths[way] > 0)
+            def _():
+                copy(way, n - 1, q).wait_recv()
+
+        for p in range(pieces):
+            lanes = slice(p * cols, (p + 1) * cols)
+            term = jnp.dot(a_ref[at, :], w_ref[me * pieces + p], preferred_element_type=F32)
+            term = term + buf[0, n - 1, at, lanes].astype(F32) + buf[1, n - 1, at, lanes].astype(F32)
+            out_ref[at, lanes] = term.astype(BF16)
+        return carry
+
+    lax.fori_loop(0, chunks, finish, 0)
+
+    def drain(index, carry):
+        slot, q = index // chunks + 1, index % chunks
+        for way, _ in ways:
+
+            @pl.when(depths[way] < slot)
+            def _():
+                copy(way, slot, q).wait_send()
+
+        return carry
+
+    lax.fori_loop(0, (n - 1) * chunks, drain, 0)
+
+
+def chain_sum(rows, gathered, n_head, chunk, part):
+    count, depth, cols = gathered.shape
+    width = count // n_head * cols
+    total = rows.shape[0]
+    return pl.pallas_call(
+        functools.partial(chain_kernel, n_head, chunk),
+        out_shape=jax.ShapeDtypeStruct((total, width), BF16),
+        in_specs=[pl.BlockSpec(memory_space=pltpu.VMEM)] * 2,
+        out_specs=pl.BlockSpec(memory_space=pltpu.VMEM),
+        scratch_shapes=[
+            pltpu.VMEM((2, n_head, total, width), BF16),
+            pltpu.SemaphoreType.DMA((2, n_head - 1, total // chunk)),
+            pltpu.SemaphoreType.DMA((2, n_head - 1, total // chunk)),
+        ],
+        compiler_params=pltpu.CompilerParams(
+            collective_id=part, has_side_effects=True, vmem_limit_bytes=56 * 2**20
+        ),
+        cost_estimate=pl.CostEstimate(
+            flops=16 * total * depth * count * cols,
+            bytes_accessed=2 * count * depth * cols,
+            transcendentals=0,
+        ),
+        name="chain_sum",
+    )(rows, gathered)
+
+
+def paired(value, bit):
+    count = lax.axis_size("seq")
+    return lax.ppermute(value, "seq", [(s, s ^ bit) for s in range(count)])
+
+
+def carry_in(finals, before, totals):
+    count = before.shape[0]
+    own = lax.axis_index("seq")
+    width = finals.shape[2]
+    half = width // 2
+    before = jnp.concatenate([before, before[-1:] + totals[-1:]], axis=0)
+
+    def at(index):
+        return lax.dynamic_index_in_dim(before, index, 0, keepdims=False)
+
+    def decay(start, end):
+        return jnp.repeat(jnp.exp(at(end) - at(start)), HEAD_DIM, axis=1)[:, None, :]
+
+    odd = own % 2
+    mine = lambda x: lax.dynamic_slice_in_dim(x, odd * half, half, 2)
+    other = paired(finals, 1)
+    own_h, other_h = mine(finals).astype(F32), mine(other).astype(F32)
+    first = jnp.where(odd == 1, other_h, own_h)
+    second = jnp.where(odd == 1, own_h, other_h)
+    pair = own - odd
+    total = mine(decay(pair + 1, pair + 2)) * first + second
+    prefix = jnp.zeros_like(total)
+    bit = 2
+    while bit < count:
+        got = paired(total.astype(BF16), bit).astype(F32)
+        upper = (own // bit) % 2 == 1
+        base = own // bit * bit
+        low = jnp.where(upper, base - bit, base)
+        prefix = jnp.where(upper, mine(decay(base, pair)) * got + prefix, prefix)
+        first = jnp.where(upper, got, total)
+        second = jnp.where(upper, total, got)
+        total = mine(decay(low + bit, low + 2 * bit)) * first + second
+        bit *= 2
+    held = prefix.astype(BF16)
+    swapped = paired(held, 1)
+    left = jnp.where(odd == 1, swapped, held)
+    right = jnp.where(odd == 1, held, swapped)
+    whole = jnp.concatenate([left, right], axis=2).astype(F32)
+    return jnp.where(odd == 1, decay(pair, pair + 1) * whole + other.astype(F32), whole)
 
 
 def per_device(
@@ -237,13 +381,11 @@
     device_logs = jnp.sum(ends, axis=-1)
     all_logs = lax.all_gather(device_logs[None], "seq", axis=0, tiled=True)
     before = jnp.cumsum(all_logs, axis=0) - all_logs
-    own = lax.axis_index("seq")
-    own_before = lax.dynamic_index_in_dim(before, own, 0, keepdims=False)
-    pieces = lax.all_gather(finals, "seq", axis=0)
-    source = jnp.arange(pieces.shape[0], dtype=jnp.int32)
-    far = jnp.where((source < own)[:, None, None], own_before[None] - before - all_logs, -jnp.inf)
-    far = jnp.repeat(jnp.exp(far), HEAD_DIM, axis=2)
-    carried = jnp.sum(far[:, :, None, :] * pieces.astype(F32), axis=0)
+    carried = carry_in(finals, before, all_logs)
+    cols = out_weight.shape[1] // 2
+    early = lax.all_gather(out_weight[:, :cols], "seq", axis=0)
+    late = lax.all_gather(out_weight[:, cols:], "seq", axis=0)
+    carried, early = lax.optimization_barrier((carried, early))
 
     block = lambda w: spec((1, SPAN, w), lambda s, g, c: (s, c, g))
     timed = spec((1, 1, SPAN, per_group), lambda s, g, c: (s, g, c, 0))
@@ -270,7 +412,13 @@
         ),
         name="span_scan",
     )(values, writes, reads, gate_inputs, ct, cr, st, et, wn, dec, carried, norm_gain[None], expand)
-    return project(normed, out_weight, n_head)
+    rows = normed.reshape(seqs * length, width)
+    chunk = rows.shape[0] // 4
+    sums = [chain_sum(rows, early, n_head, chunk, 0)]
+    rows, sums[0] = lax.optimization_barrier((rows, sums[0]))
+    sums.append(chain_sum(rows, late, n_head, chunk, 1))
+    sums = [x.reshape(seqs, length, -1, cols) for x in sums]
+    return jnp.concatenate(sums, axis=3).reshape(seqs, length, -1)
 
 
 def solution(mesh):

time: 646 us -> 476 us (0.74); the launches traced: 636 us -> 474 us
  Pallas kernels: 39.7 us -> 335 us
  waiting for transfers between devices: 337 us -> 49.7 us
  matrix products: 138 us -> 0 us
  starting transfers between devices: 45.9 us -> 11.7 us
  local copies, waits for them, and re-layouts: 10.7 us -> 37.1 us
  other arithmetic: 40.9 us -> 17.6 us
    pallas_call x0 -> x2, Pallas kernels: none -> 296 us  [chain_sum(): pl.pallas_call(functools.partial(chain_kernel, n_head, chunk), out_shape=...]
    all_gather x2, waiting for transfers between devices: 173 us -> 0.04 us  [the longest x1 0.02 us: per_device(): early = lax.all_gather(out_weight[:, :cols], 'seq', axis=0)]
    dot_general x28 -> x0, matrix products: 138 us -> none  [partial(): jnp.dot(rows, cut[p], preferred_element_type=F32)]
    ppermute x12 -> x4, waiting for transfers between devices: 163 us -> 48.9 us  [paired(): return lax.ppermute(value, 'seq', [(s, s ^ bit) for s in range(count)])]
    ppermute x12 -> x4, starting transfers between devices: 37.1 us -> 2.88 us  [paired(): return lax.ppermute(value, 'seq', [(s, s ^ bit) for s in range(count)])]
    convert_element_type x8 -> x3, other arithmetic: 23.8 us -> 0.91 us  [the longest x2 0.65 us: carry_in(): got = paired(total.astype(BF16), bit).astype(F32)]
    reshape x0 -> x3, local copies, waits for them, and re-layouts: none -> 15.6 us  [the longest x2 7.79 us: per_device(): sums = [x.reshape(seqs, length, -1, cols) for x in sums]]
    concatenate x4 -> x1, other arithmetic: 0.72 us -> 7.31 us  [per_device(): return jnp.concatenate(sums, axis=3).reshape(seqs, length, -1)]
  transfers between devices with their start and end apart: 17 -> 9, of which waited for: 8 -> 2; matrix products, arithmetic and copies ran while one was open for 15% -> 5% of each run, Pallas kernels for 4% -> 39%
where the time goes in v2:
time: 476 us; the launch traced here: 474 us
  Pallas kernels  335 us (70%)
  waiting for transfers between devices  49.7 us (10%)
  local copies, waits for them, and re-layouts  37.1 us (8%)
  other arithmetic  17.6 us (4%)
  between operations  13.9 us (3%)
  starting transfers between devices  11.7 us (2%)
  blocking collectives  8.87 us (2%)
    pallas_call x2, Pallas kernels, chain_sum(): pl.pallas_call(functools.partial(chain_kernel, n_head, chunk), out_shape=...  296 us
    ppermute x4, waiting for transfers between devices, paired(): return lax.ppermute(value, 'seq', [(s, s ^ bit) for s in range(count)])  48.9 us
    pallas_call x1, Pallas kernels, per_device(): pl.pallas_call(functools.partial(scan_kernel, per_group), grid=(seqs, gro...  26.3 us
    pallas_call x1, Pallas kernels, per_device(): pl.pallas_call(local_kernel, grid=(seqs, groups), in_specs=[tall(gw), tal...  13 us
  transfers between devices with their start and end apart: 9, of which 2 were waited for; matrix products, arithmetic and copies ran while one was open for 5% of the time, Pallas kernels for 39%

profile of v2, /device:TPU:0, one launch (start us, length us, event | category | flops | bytes accessed | tf_op | source)
XLA Modules:
  0.0 473.8 jit_solution(756956405915021471)
XLA Ops:
  6.5 4.4 fusion.24
  11.7 1.6 slice.24
  13.3 2.4 collective-permute-start
  15.7 4.5 collective-permute-start.1
  20.8 1.9 collective-permute-start.2
  23.5 2.3 reduce_window_sum.35
  25.8 0.8 slice_reduce_fusion
  29.8 1.2 copy.58
  31.0 2.2 copy.52
  33.2 2.3 fusion.10
  35.6 13.0 %local_states.1 = (bf16[2,512,2048]{2,1,0:T(8,128)(2,1)}, bf16[2,512,256]{2,1,0:T(8,128)(2,1)S(1)}, bf16[2,512,256]{2,1,0:T(8,128)(2,1)S(1)}, bf16[2,128,2048]{2,1,0:T(8,128)(2,1)S(1)}) custom-call(bf16[2,512,2048]{2,1,0:T(8,128)(2,1)} %x_ref.1, bf16[2,512,256]{2,1,0:T(8,128)(2,1)S(1)} %copy-done.2, bf16[2,512,256]{2,1,0:T(8,128)(2,1)S(1)} %copy-done.3, ...), custom_call_target="tpu_custom_call" | custom-call | flops 1073741824 | bytes 8388608 | tf_op jit(solution)/shard_map/local_states/pallas_call | solution.py:353
  48.6 0.8 copy-done.4
  49.4 0.8 copy-done.6
  50.2 1.6 collective-permute-start.3
  51.8 8.9 %all-gather.3 = f32[8,2,32]{2,1,0:T(2,128)S(1)} all-gather(f32[1,2,32]{2,1,0:T(2,128)S(1)} %bitcast.61), channel_id=2, replica_groups=mesh['seq'=8,'head'=4] {'seq'}, dimensions={0}, use_global_device_ids=true | all-gather | bytes 2304 | tf_op jit(solution)/shard_map/all_gather | solution.py:382
  62.0 25.1 %collective-permute-done.4 = bf16[2,128,1024]{2,1,0:T(8,128)(2,1)S(1)} collective-permute-done((bf16[2,128,1024]{2,1,0:T(8,128)(2,1)S(1)}, bf16[2,128,1024]{2,1,0:T(8,128)(2,1)S(1)}, u32[]{:S(2)}, u32[]{:S(2)}) %collective-permute-start.4) | collective-permute-done | bytes 524320 | tf_op jit(solution)/shard_map/ppermute | solution.py:250
  88.5 23.9 %collective-permute-done.5 = bf16[2,128,1024]{2,1,0:T(8,128)(2,1)S(1)} collective-permute-done((bf16[2,128,1024]{2,1,0:T(8,128)(2,1)S(1)}, bf16[2,128,1024]{2,1,0:T(8,128)(2,1)S(1)}, u32[]{:S(2)}, u32[]{:S(2)}) %collective-permute-start.5) | collective-permute-done | bytes 524320 | tf_op jit(solution)/shard_map/ppermute | solution.py:250
  112.7 1.3 copy.53
  114.2 1.0 copy.56
  115.2 0.8 broadcast_in_dim.34
  116.3 1.6 convert_select_fusion.carry_ref
  118.0 1.0 copy-done
  119.0 1.0 copy-done.1
  120.0 1.0 copy-done.5
  121.1 1.0 copy-done.7
  122.1 26.3 %span_scan.1 = bf16[2,512,2048]{2,1,0:T(8,128)(2,1)} custom-call(bf16[2,512,2048]{2,1,0:T(8,128)(2,1)} %get-tuple-element.13.v_ref, bf16[2,512,256]{2,1,0:T(8,128)(2,1)S(1)} %copy-done.5, bf16[2,512,256]{2,1,0:T(8,128)(2,1)S(1)} %copy-done.7, bf16[2,512,2048]{2,1,0:T(8,128)(2,1)} %gate_ref.1, f32[2,2,512,16]{3,2,1,0:T(8,128)S(1)} %bitcast.50, ...), custom_call_target="tpu_custom_call" | custom-call | flops 2147483648 | bytes 12582912 | tf_op jit(solution)/shard_map/span_scan/pallas_call | solution.py:393
  148.4 147.0 %chain_sum.2 = bf16[1024,1024]{1,0:T(8,128)(2,1)} custom-call(bf16[1024,2048]{1,0:T(8,128)(2,1)} %bitcast.55, bf16[8,2048,512]{2,1,0:T(8,128)(2,1)} %bitcast.62), custom_call_target="tpu_custom_call" | custom-call | flops 137438953472 | bytes 16777216 | tf_op jit(solution)/shard_map/chain_sum/pallas_call | solution.py:226
  295.5 148.6 %chain_sum.3 = bf16[1024,1024]{1,0:T(8,128)(2,1)} custom-call(bf16[1024,2048]{1,0:T(8,128)(2,1)} %bitcast.56, bf16[8,2048,512]{2,1,0:T(8,128)(2,1)} %bitcast.63), custom_call_target="tpu_custom_call" | custom-call | flops 137438953472 | bytes 16777216 | tf_op jit(solution)/shard_map/chain_sum/pallas_call | solution.py:226
  444.0 3.3 reshape.94
  447.4 4.5 reshape.93
  451.8 7.3 %pad_maximum_fusion = bf16[2,512,2,1024]{3,2,1,0:T(2,128)(2,1)} fusion(bf16[2,512,2,512]{3,2,1,0:T(2,128)(2,1)S(1)} %reshape.94, bf16[2,512,2,512]{3,2,1,0:T(2,128)(2,1)} %reshape.93), kind=kLoop, calls=%fused_computation | loop fusion | flops 8388608 | bytes 8388608 | tf_op jit(solution)/shard_map/concatenate | solution.py:421
  459.2 7.8 %reshape.95 = bf16[2,512,2048]{2,1,0:T(8,128)(2,1)} reshape(bf16[2,512,2,1024]{3,2,1,0:T(2,128)(2,1)} %pad_maximum_fusion) | data formatting | bytes 8388608 | tf_op jit(solution)/shard_map/reshape | solution.py:421
  (92 shorter events, 8.6 us)
Async XLA Ops:
  6.5 111.4 %all-gather.7.cloned.1.call-start = ((), (), s32[]{:S(2)}) async-start(), calls=%async_computation | async-start | bytes 18874368 | tf_op jit(solution)/shard_map/all_gather | solution.py:386
  10.9 4.7 %copy-start.2 = (bf16[2,512,256]{2,1,0:T(8,128)(2,1)S(1)}, bf16[2,512,256]{2,1,0:T(8,128)(2,1)}, u32[]{:S(2)}) copy-start(bf16[2,512,256]{2,1,0:T(8,128)(2,1)} %w_ref.1) | copy-start | bytes 1572868
  11.0 9.3 %copy-start.3 = (bf16[2,512,256]{2,1,0:T(8,128)(2,1)S(1)}, bf16[2,512,256]{2,1,0:T(8,128)(2,1)}, u32[]{:S(2)}) copy-start(bf16[2,512,256]{2,1,0:T(8,128)(2,1)} %r_ref.1) | copy-start | bytes 1572868
  11.0 11.8 %copy-start.17 = (f32[32]{0:T(128)S(1)}, f32[32]{0:T(128)}, u32[]{:S(2)}) copy-start(f32[32]{0:T(128)} %param.16) | copy-start | bytes 388
  11.0 11.8 %copy-start.15 = (f32[2,32,512]{2,1,0:T(8,128)S(1)}, f32[2,32,512]{2,1,0:T(8,128)}, u32[]{:S(2)}) copy-start(f32[2,32,512]{2,1,0:T(8,128)} %param.15) | copy-start | bytes 393220
  11.0 284.5 %all-gather.9.cloned.1.call-start = ((), (), s32[]{:S(2)}) async-start(), calls=%async_computation.1 | async-start | bytes 18874368 | tf_op jit(solution)/shard_map/all_gather | solution.py:387
  13.3 22.2 %collective-permute-start = (bf16[2,16,2048]{2,1,0:T(8,128)(2,1)}, bf16[2,16,2048]{2,1,0:T(8,128)(2,1)S(1)}, u32[]{:S(2)}, u32[]{:S(2)}) collective-permute-start(bf16[2,16,2048]{2,1,0:T(8,128)(2,1)} %slice.24), channel_id=1, source_target_pairs={{0,4},{4,8},{8,12},{12,16},{16,20},{20,24},{24,28},{1,5},{5,9},{9,... | collective-permute-start | bytes 393224 | tf_op jit(solution)/shard_map/ppermute | solution.py:24
  15.7 19.8 %collective-permute-start.1 = (bf16[2,16,256]{2,1,0:T(8,128)(2,1)S(1)}, bf16[2,16,256]{2,1,0:T(8,128)(2,1)S(1)}, u32[]{:S(2)}, u32[]{:S(2)}) collective-permute-start(bf16[2,16,256]{2,1,0:T(8,128)(2,1)S(1)} %slice.25), channel_id=1, source_target_pairs={{0,4},{4,8},{8,12},{12,16},{16,20},{20,24},{24,28},{1,5},{5,9},{9,... | collective-permute-start | bytes 49160 | tf_op jit(solution)/shard_map/ppermute | solution.py:24
  20.8 14.7 %collective-permute-start.2 = (bf16[2,16,256]{2,1,0:T(8,128)(2,1)}, bf16[2,16,256]{2,1,0:T(8,128)(2,1)S(1)}, u32[]{:S(2)}, u32[]{:S(2)}) collective-permute-start(bf16[2,16,256]{2,1,0:T(8,128)(2,1)} %slice.26), channel_id=1, source_target_pairs={{0,4},{4,8},{8,12},{12,16},{16,20},{20,24},{24,28},{1,5},{5,9},{9,... | collective-permute-start | bytes 49160 | tf_op jit(solution)/shard_map/ppermute | solution.py:24
  28.7 0.7 copy-start.14
  33.2 2.3 copy-start.8
  33.2 2.3 copy-start.10
  33.2 2.3 copy-start.11
  35.6 16.3 %copy-start.16 = (f32[2,32]{1,0:T(2,128)S(1)}, f32[2,32]{1,0:T(2,128)}, u32[]{:S(2)}) copy-start(f32[2,32]{1,0:T(2,128)} %get-tuple-element.21) | copy-start | bytes 772
  48.6 0.8 copy-start.4
  49.4 0.8 copy-start.6
  50.2 10.8 %collective-permute-start.3 = (bf16[2,128,2048]{2,1,0:T(8,128)(2,1)S(1)}, bf16[2,128,2048]{2,1,0:T(8,128)(2,1)S(1)}, u32[]{:S(2)}, u32[]{:S(2)}) collective-permute-start(bf16[2,128,2048]{2,1,0:T(8,128)(2,1)S(1)} %get-tuple-element.16), channel_id=1, source_target_pairs={{0,4},{4,0},{8,12},{12,8},{16,20},{20,16},{24,28},{28,24},{1,5},{5... | collective-permute-start | bytes 3145736 | tf_op jit(solution)/shard_map/ppermute | solution.py:250
  61.0 51.6 %copy-start.12 = (bf16[2,128,2048]{2,1,0:T(8,128)(2,1)}, bf16[2,128,2048]{2,1,0:T(8,128)(2,1)S(1)}, u32[]{:S(2)}) copy-start(bf16[2,128,2048]{2,1,0:T(8,128)(2,1)S(1)} %collective-permute-done.3) | copy-start | bytes 3145732
  61.3 25.8 %collective-permute-start.4 = (bf16[2,128,1024]{2,1,0:T(8,128)(2,1)S(1)}, bf16[2,128,1024]{2,1,0:T(8,128)(2,1)S(1)}, u32[]{:S(2)}, u32[]{:S(2)}) collective-permute-start(bf16[2,128,1024]{2,1,0:T(8,128)(2,1)S(1)} %fusion.8), channel_id=1, source_target_pairs={{0,8},{4,12},{8,0},{12,4},{16,24},{20,28},{24,16},{28,20},{1,9},{5... | collective-permute-start | bytes 1572872 | tf_op jit(solution)/shard_map/ppermute | solution.py:250
  62.0 52.0 %copy-start.13 = (f32[2,32,512]{2,1,0:T(8,128)S(1)}, f32[2,32,512]{2,1,0:T(8,128)}, u32[]{:S(2)}) copy-start(f32[2,32,512]{2,1,0:T(8,128)} %get-tuple-element.35) | copy-start | bytes 393220
  87.5 24.9 %collective-permute-start.5 = (bf16[2,128,1024]{2,1,0:T(8,128)(2,1)S(1)}, bf16[2,128,1024]{2,1,0:T(8,128)(2,1)S(1)}, u32[]{:S(2)}, u32[]{:S(2)}) collective-permute-start(bf16[2,128,1024]{2,1,0:T(8,128)(2,1)S(1)} %fusion.5), channel_id=1, source_target_pairs={{0,16},{4,20},{8,24},{12,28},{16,0},{20,4},{24,8},{28,12},{1,17},{... | collective-permute-start | bytes 1572872 | tf_op jit(solution)/shard_map/ppermute | solution.py:250
  112.6 3.5 collective-permute-start.6
  116.3 1.7 copy-start.9
  117.9 1.0 copy-start
  119.0 1.0 copy-start.1
  120.0 1.0 copy-start.5
  121.1 1.0 copy-start.7
Sparse Core Ops, SparseCore 0:
  11.1 104.2 all-gather.6
  117.3 89.9 all-gather.8
